TPU v7x, 512 devices: a whole 4x8x8 slice. The times are simulated.
512 devices in a mesh: section: 16 (over y, z_hi), dp: 16 (over z_lo, x), cores: 2 (over core).
Axes of the slice: x: 4, y: 8, z: 8 (z_hi: 2, z_lo: 4; z = z_hi * 4 + z_lo), core: 2. Of those that a mesh axis runs over, the one named last changes fastest.
Arguments:
- arrivals: bfloat16 [2, 1536, 2048], P(None, 'dp'), may hold values from -6 to 6
- in_flight: bfloat16 [16, 1536, 2048], P('section', 'dp'), may hold values from -6 to 6
- cotangent: bfloat16 [2, 1536, 2048], P(None, 'dp'), may hold values from -6 to 6
- grad_flight: bfloat16 [16, 1536, 2048], P('section', 'dp'), may hold values from -6 to 6
- stashed: bfloat16 [16, 2, 1536, 2048], P('section', None, 'dp'), may hold values from -6 to 6
- in_weight: bfloat16 [16, 2048, 4096], P('section', 'dp', 'cores'), may hold values from -0.125 to 0.125
- out_weight: bfloat16 [16, 1024, 2048], P('section', 'cores', 'dp'), may hold values from -0.1875 to 0.1875
- forward_blocks: int32 [16, 17], P('dp'), may hold values from 1 to 4, 42 in all within a row
- backward_blocks: int32 [16, 17], P('dp'), may hold values from 1 to 4, 42 in all within a row
- forward_marks: int32 [16, 17, 4, 4], P('dp'), may hold values 0 or 1
- backward_marks: int32 [16, 17, 4, 4], P('dp'), may hold values 0 or 1
Outputs:
- activations: bfloat16 [16, 2, 1536, 2048], P('section', None, ('dp', 'cores'))
- input_grads: bfloat16 [16, 2, 1536, 2048], P('section', None, ('dp', 'cores'))
- weight_grads: float32 [16, 1024, 2048], P('section', 'cores', 'dp')
Inputs may be any that keep to these rules, and one draw needn't show every extreme that they name: `forward_blocks`: in each replica's row the 17 lengths add up to 42 blocks and the longest is 4. `backward_blocks`: in each replica's row the 17 lengths add up to 42 blocks and the longest is 4.
All inputs are finite; a program needn't handle non-finite values. No bound on the sum of `forward_marks` or of `backward_marks` on one device may be relied on, other than what follows from the above.
Results may differ from a plain program's by a relative error of at most 0.03.
Values may be sent and summed in bfloat16 or wider, within the bound.
A program may use at most 64 MiB of HBM per device.

v0:
```python
import jax
import jax.numpy as jnp
from jax import lax
from jax.sharding import PartitionSpec as P

HEAD_DIM = 128
BLOCK = 24
BLOCKS = 4
EPSILON = 1e-06


def from_behind(x, axis, by):
    peers = lax.axis_size(axis)
    pairs = [(i, i + by) for i in range(peers) if 0 <= i + by < peers]
    return lax.ppermute(x, axis, pairs)


def block_keep(live_blocks, block_marks):
    length = BLOCKS * BLOCK
    places = jnp.arange(length, dtype=jnp.int32)
    owners = places // BLOCK
    onehot = (owners[:, None] == jnp.arange(BLOCKS, dtype=jnp.int32)[None, :]).astype(jnp.float32)
    spread = jnp.einsum("ia,rab,jb->rij", onehot, block_marks.astype(jnp.float32), onehot)
    allowed = (owners[:, None] == owners[None, :])[None] | (spread > 0.5)
    causal = (places[:, None] >= places[None, :])[None]
    tokens_live = live_blocks * BLOCK
    living = places[None, :] < tokens_live[:, None]
    keeping = causal & allowed & living[:, :, None] & living[:, None, :]
    return (keeping.astype(jnp.float32), 1.0 / tokens_live.astype(jnp.float32))


def choose_history(block_table, mark_table, history):
    histories = block_table.shape[1]
    matches = jnp.arange(histories, dtype=jnp.int32) == history
    blocks = jnp.sum(jnp.where(matches, block_table[0], 0))
    marked = jnp.sum(jnp.where(matches[:, None, None], mark_table[0], 0), axis=0)
    return block_keep(blocks[None], marked[None])


def norm_rows(values_f):
    return lax.rsqrt(jnp.mean(values_f * values_f, axis=-1, keepdims=True) + EPSILON)


def heads_forward(pre_act, keeping, inverse_count):
    scaling = HEAD_DIM ** (-0.5)
    active = jax.nn.silu(pre_act)
    gate_rows = active[:, :, :, 0]
    value_rows = active[:, :, :, 1].astype(jnp.bfloat16)
    query_rows = active[:, :, :, 2].astype(jnp.bfloat16)
    key_rows = active[:, :, :, 3].astype(jnp.bfloat16)
    scores = (
        jnp.einsum("rigd,rjgd->rgij", query_rows, key_rows, preferred_element_type=jnp.float32)
        * scaling
    )
    weights = keeping[:, None] * inverse_count[:, None, None, None]
    attention = (jax.nn.silu(scores) * weights).astype(jnp.bfloat16)
    mixed = jnp.einsum("rgij,rjgd->rigd", attention, value_rows, preferred_element_type=jnp.float32)
    root_scale = lax.rsqrt(jnp.mean(mixed * mixed, axis=-1, keepdims=True) + EPSILON)
    normed = mixed * root_scale
    gated = (normed * gate_rows).astype(jnp.bfloat16)
    return (
        gated,
        (
            gate_rows,
            value_rows,
            query_rows,
            key_rows,
            scores,
            weights,
            attention,
            root_scale,
            normed,
        ),
    )


def heads_backward(pre_act, saved, upstream):
    gate_rows, value_rows, query_rows, key_rows, scores, weights, attention, root_scale, normed = (
        saved
    )
    scaling = HEAD_DIM ** (-0.5)
    grad_gated = upstream.astype(jnp.float32)
    grad_normed = grad_gated * gate_rows
    grad_gate = grad_gated * normed
    grad_mixed = root_scale * (
        grad_normed - normed * jnp.mean(grad_normed * normed, axis=-1, keepdims=True)
    )
    mixed_low = grad_mixed.astype(jnp.bfloat16)
    grad_attention = jnp.einsum(
        "rigd,rjgd->rgij", mixed_low, value_rows, preferred_element_type=jnp.float32
    )
    grad_value = jnp.einsum(
        "rgij,rigd->rjgd", attention, mixed_low, preferred_element_type=jnp.float32
    )
    sigmoid_s = jax.nn.sigmoid(scores)
    grad_scores = (
        grad_attention * weights * sigmoid_s * (1.0 + scores * (1.0 - sigmoid_s)) * scaling
    ).astype(jnp.bfloat16)
    grad_query = jnp.einsum(
        "rgij,rjgd->rigd", grad_scores, key_rows, preferred_element_type=jnp.float32
    )
    grad_key = jnp.einsum(
        "rgij,rigd->rjgd", grad_scores, query_rows, preferred_element_type=jnp.float32
    )
    grad_active = jnp.stack([grad_gate, grad_value, grad_query, grad_key], axis=3)
    sigmoid_u = jax.nn.sigmoid(pre_act)
    return (grad_active * sigmoid_u * (1.0 + pre_act * (1.0 - sigmoid_u))).astype(jnp.bfloat16)


def per_device(
    arrivals,
    in_flight,
    cotangent,
    grad_flight,
    stashed,
    in_weight,
    out_weight,
    forward_blocks,
    backward_blocks,
    forward_marks,
    backward_marks,
):
    section_no = lax.axis_index("section")
    sections = lax.axis_size("section")
    core_no = lax.axis_index("cores")
    ticks = arrivals.shape[0]
    length = arrivals.shape[1]
    share = length // lax.axis_size("cores")
    row_start = core_no * share
    out_full = lax.all_gather(out_weight[0], "dp", axis=1, tiled=True)
    slab_rows = out_full.shape[0]
    groups = slab_rows // HEAD_DIM
    columns = in_weight.shape[2]
    in_full = None
    in_full = lax.all_gather(in_weight[0], "dp", axis=0, tiled=True)
    received = in_flight[0]
    returned = grad_flight[0]
    ahead_out = []
    back_out = []
    gated_list = []
    upstream_list = []
    for tick_no in range(ticks):
        if tick_no == 0:
            prior = in_flight[0]
            later = grad_flight[0]
        else:
            prior = received
            later = returned
        inputs = jnp.where(section_no == 0, arrivals[tick_no], prior)
        upstream = jnp.where(section_no == sections - 1, cotangent[tick_no], later)
        keep_ahead, count_ahead = choose_history(
            forward_blocks, forward_marks, tick_no - section_no + sections - 1
        )
        keep_back, count_back = choose_history(
            backward_blocks, backward_marks, tick_no + section_no
        )
        floats = inputs.astype(jnp.float32)
        saved_floats = stashed[0, tick_no].astype(jnp.float32)
        root_saved = norm_rows(saved_floats)
        scaled_saved = saved_floats * root_saved
        both_normed = jnp.concatenate(
            [(floats * norm_rows(floats)).astype(jnp.bfloat16), scaled_saved.astype(jnp.bfloat16)],
            axis=0,
        )
        pre_both = jnp.dot(both_normed, in_full, preferred_element_type=jnp.float32)
        pre_ahead = pre_both[:length].reshape(1, length, groups, 4, HEAD_DIM)
        pre_back = pre_both[length:].reshape(1, length, groups, 4, HEAD_DIM)
        gated_ahead, unused = heads_forward(pre_ahead, keep_ahead, count_ahead)
        partial_sum = jnp.dot(
            gated_ahead.reshape(length, slab_rows), out_full, preferred_element_type=jnp.float32
        )
        summed = lax.psum(partial_sum.astype(jnp.bfloat16), "cores").astype(jnp.float32)
        outgoing = (floats + summed).astype(jnp.bfloat16)
        ahead_out.append(lax.dynamic_slice_in_dim(outgoing, row_start, share, 0))
        if tick_no + 1 < ticks:
            received = from_behind(outgoing, "section", 1)
        gated_back, saved = heads_forward(pre_back, keep_back, count_back)
        grad_gated = (
            jnp.einsum("sd,fd->sf", upstream, out_full, preferred_element_type=jnp.float32)
            .astype(jnp.bfloat16)
            .reshape(1, length, groups, HEAD_DIM)
        )
        grad_pre = heads_backward(pre_back, saved, grad_gated).reshape(length, columns)
        grad_normed = jnp.einsum("sf,df->sd", grad_pre, in_full, preferred_element_type=jnp.float32)
        back_part = root_saved * (
            grad_normed
            - scaled_saved * jnp.mean(grad_normed * scaled_saved, axis=-1, keepdims=True)
        )
        back_sum = lax.psum(back_part.astype(jnp.bfloat16), "cores").astype(jnp.float32)
        grad_in = (upstream.astype(jnp.float32) + back_sum).astype(jnp.bfloat16)
        back_out.append(lax.dynamic_slice_in_dim(grad_in, row_start, share, 0))
        gated_list.append(gated_back.reshape(length, slab_rows))
        upstream_list.append(upstream)
        if tick_no + 1 < ticks:
            returned = from_behind(grad_in, "section", -1)
    stacked_gated = jnp.concatenate(gated_list, axis=0)
    stacked_upstream = jnp.concatenate(upstream_list, axis=0)
    product = lax.dot_general(
        stacked_gated,
        stacked_upstream,
        (((0,), (0,)), ((), ())),
        preferred_element_type=jnp.float32,
    )
    scaling = (ticks * length * lax.axis_size("dp")) ** (-0.5)
    grads_sum = (
        lax.psum_scatter(
            product.astype(jnp.bfloat16), "dp", scatter_dimension=1, tiled=True
        ).astype(jnp.float32)
        * scaling
    )
    return (jnp.stack(ahead_out)[None], jnp.stack(back_out)[None], grads_sum[None])


def solution(mesh):
    in_specs = (
        P(None, "dp", None),
        P("section", "dp", None),
        P(None, "dp", None),
        P("section", "dp", None),
        P("section", None, "dp", None),
        P("section", "dp", "cores"),
        P("section", "cores", "dp"),
        P("dp", None),
        P("dp", None),
        P("dp", None, None, None),
        P("dp", None, None, None),
    )
    out_specs = (
        P("section", None, ("dp", "cores"), None),
        P("section", None, ("dp", "cores"), None),
        P("section", "cores", "dp"),
    )
    return jax.shard_map(
        per_device, mesh=mesh, in_specs=in_specs, out_specs=out_specs, check_vma=False
    )
```

profile of v0, /device:TPU:8, one launch (start us, length us, event | category | flops | bytes accessed | tf_op | source)
XLA Modules:
  0.0 493.3 jit_solution(5450123814144851031)
XLA Ops:
  18.4 73.2 %all-gather.7.cloned.1.call-done = bf16[1,512,2048]{2,1,0:T(8,128)(2,1)} async-done(((bf16[1,512,128]{2,1,0:T(8,128)(2,1)}), bf16[1,512,2048]{2,1,0:T(8,128)(2,1)}) %all-gather.7.cloned.1.call-update) | async-done | bytes 2097168 | tf_op jit(solution)/shard_map/all_gather | solution.py:130
  91.6 2.4 fusion.31
  94.7 104.7 %all-gather.5.cloned.1.call-done = bf16[1,2048,2048]{2,1,0:T(8,128)(2,1)} async-done(((bf16[1,128,2048]{2,1,0:T(8,128)(2,1)}), bf16[1,2048,2048]{2,1,0:T(8,128)(2,1)}) %all-gather.5.cloned.1.call-update) | async-done | bytes 8388624 | tf_op jit(solution)/shard_map/all_gather | solution.py:135
  199.4 5.2 %fusion.6 = f32[192,2048]{1,0:T(8,128)S(1)} fusion(bf16[1,2048,2048]{2,1,0:T(8,128)(2,1)} %all-gather.5.cloned.1.call-done, bf16[96,2048]{1,0:T(8,128)(2,1)S(1)} %get-tuple-element.54, bf16[96,2048]{1,0:T(8,128)(2,1)S(1)} %get-tuple-element.55), kind=kOutput, calls=%fused_computation.6 | convolution fusion | flops 1612185600 | bytes 10747904 | tf_op jit(solution)/shard_map/dot_general | solution.py:165
  216.6 6.5 %fusion.68 = (f32[96]{0:T(128)S(1)}, f32[96]{0:T(128)S(1)}, f32[96,2048]{1,0:T(8,128)S(1)}) fusion(f32[96]{0:T(128)S(1)} %add_rsqrt_fusion.6, bf16[1,2,96,2048]{3,2,1,0:T(8,128)(2,1)S(1)} %copy-done.1, bf16[1,2048,2048]{2,1,0:T(8,128)(2,1)} %all-gather.5.cloned.1.call-done, f32[96,2048]{1,0:T(8,128)} %stack.60, f32[192,2048]{1,0:T(8,128)S(1)} %copy-done.10), kind=kOutput, calls=%fused_computation.86 | convolution fusion | flops 808451840 | bytes 11535616 | tf_op jit(solution)/shard_map/sf,df->sd/dot_general | solution.py:184
  228.6 30.0 %all-reduce.7.cloned.1.call-done = (bf16[96,2048]{1,0:T(8,128)(2,1)}, bf16[96,2048]{1,0:T(8,128)(2,1)}) async-done(((bf16[96,2048]{1,0:T(8,128)(2,1)}, bf16[96,2048]{1,0:T(8,128)(2,1)}), (bf16[96,2048]{1,0:T(8,128)(2,1)}, bf16[96,2048]{1,0:T(8,128)(2,1)})) %all-reduce.7.cloned.1.call-update) | async-done | bytes 786448 | tf_op jit(solution)/shard_map/psum | solution.py:172
  259.8 8.1 %collective-permute-start = (bf16[96,2048]{1,0:T(8,128)(2,1)S(1)}, bf16[96,2048]{1,0:T(8,128)(2,1)S(1)}, u32[]{:S(2)}, u32[]{:S(2)}) collective-permute-start(bf16[96,2048]{1,0:T(8,128)(2,1)S(1)} %fusion.80), channel_id=1, source_target_pairs={{0,32},{32,64},{64,96},{96,128},{128,160},{160,192},{192,224},{224... | collective-permute-start | bytes 1179656 | tf_op jit(solution)/shard_map/ppermute | solution.py:15
  267.9 1.9 add_convert_fusion
  269.8 2.8 collective-permute-start.1
  272.6 26.8 %collective-permute-done = bf16[96,2048]{1,0:T(8,128)(2,1)S(1)} collective-permute-done((bf16[96,2048]{1,0:T(8,128)(2,1)S(1)}, bf16[96,2048]{1,0:T(8,128)(2,1)S(1)}, u32[]{:S(2)}, u32[]{:S(2)}) %collective-permute-start) | collective-permute-done | bytes 393248 | tf_op jit(solution)/shard_map/ppermute | solution.py:15
  299.8 5.2 %fusion.4 = f32[192,2048]{1,0:T(8,128)S(1)} fusion(bf16[1,2048,2048]{2,1,0:T(8,128)(2,1)} %all-gather.5.cloned.1.call-done, bf16[96,2048]{1,0:T(8,128)(2,1)S(1)} %copy-done.21, bf16[96,2048]{1,0:T(8,128)(2,1)S(1)} %multiply_convert_fusion.2), kind=kOutput, calls=%fused_computation.4 | convolution fusion | flops 1612185600 | bytes 10747904 | tf_op jit(solution)/shard_map/dot_general | solution.py:165
  307.5 2.5 reshape.826
  310.0 2.4 fusion.152
  315.3 1.5 fusion.28
  317.8 1.9 multiply_convert_fusion.5
  324.8 2.6 reshape.822
  327.4 2.5 fusion.153
  329.9 2.0 multiply_reduce_fusion.5
  336.3 2.4 stack.67
  338.7 6.8 %fusion.73 = (f32[96]{0:T(128)S(1)}, f32[96,2048]{1,0:T(8,128)S(1)}) fusion(f32[96]{0:T(128)S(1)} %add_rsqrt_fusion.4, bf16[1,2,96,2048]{3,2,1,0:T(8,128)(2,1)} %param.15, bf16[1,2048,2048]{2,1,0:T(8,128)(2,1)} %all-gather.5.cloned.1.call-done, f32[96,2048]{1,0:T(8,128)} %stack.67, f32[192,2048]{1,0:T(8,128)} %copy-done.8), kind=kOutput, calls=%fused_computation.91 | convolution fusion | flops 807862144 | bytes 11141888 | tf_op jit(solution)/shard_map/sf,df->sd/dot_general | solution.py:184
  347.9 1.7 convolution_convert_fusion
  349.7 2.5 copy.74
  354.2 35.7 %all-reduce.5.cloned.1.call-done = (bf16[96,2048]{1,0:T(8,128)(2,1)}, bf16[96,2048]{1,0:T(8,128)(2,1)}) async-done(((bf16[96,2048]{1,0:T(8,128)(2,1)}, bf16[96,2048]{1,0:T(8,128)(2,1)}), (bf16[96,2048]{1,0:T(8,128)(2,1)}, bf16[96,2048]{1,0:T(8,128)(2,1)})) %all-reduce.5.cloned.1.call-update) | async-done | bytes 786448 | tf_op jit(solution)/shard_map/psum | solution.py:172
  393.4 91.7 %reduce-scatter.4.cloned.1.call-done = bf16[128,512]{1,0:T(8,128)(2,1)} async-done(((bf16[2048,512]{1,0:T(8,128)(2,1)}), bf16[128,512]{1,0:T(8,128)(2,1)}) %reduce-scatter.4.cloned.1.call-update) | async-done | bytes 131088
  (156 shorter events, 53.2 us)
Async XLA Ops:
  7.2 11.0 %copy-start.1 = (bf16[1,2,96,2048]{3,2,1,0:T(8,128)(2,1)S(1)}, bf16[1,2,96,2048]{3,2,1,0:T(8,128)(2,1)}, u32[]{:S(2)}) copy-start(bf16[1,2,96,2048]{3,2,1,0:T(8,128)(2,1)} %param.15) | copy-start | bytes 2359300
  7.2 10.9 %copy-start.24 = (bf16[1,96,2048]{2,1,0:T(8,128)(2,1)S(1)}, bf16[1,96,2048]{2,1,0:T(8,128)(2,1)}, u32[]{:S(2)}) copy-start(bf16[1,96,2048]{2,1,0:T(8,128)(2,1)} %param.14) | copy-start | bytes 1179652
  7.2 10.9 %copy-start.17 = (bf16[2,96,2048]{2,1,0:T(8,128)(2,1)S(1)}, bf16[2,96,2048]{2,1,0:T(8,128)(2,1)}, u32[]{:S(2)}) copy-start(bf16[2,96,2048]{2,1,0:T(8,128)(2,1)} %param.13) | copy-start | bytes 2359300
  7.2 84.4 %all-gather.7.cloned.1.call-start = ((), (), s32[]{:S(2)}) async-start(), calls=%async_computation.2 | async-start | bytes 2228224 | tf_op jit(solution)/shard_map/all_gather | solution.py:130
  7.9 191.5 %all-gather.5.cloned.1.call-start = ((), (), s32[]{:S(2)}) async-start(), calls=%async_computation.1 | async-start | bytes 8912896 | tf_op jit(solution)/shard_map/all_gather | solution.py:135
  8.7 249.9 %all-reduce.7.cloned.1.call-start = ((), (), s32[]{:S(2)}) async-start(), calls=%async_computation.5 | async-start | bytes 1572864 | tf_op jit(solution)/shard_map/psum | solution.py:172
  16.0 78.0 %copy-start.5 = (bf16[1,96,2048]{2,1,0:T(8,128)(2,1)}, bf16[1,96,2048]{2,1,0:T(8,128)(2,1)S(1)}, u32[]{:S(2)}) copy-start(bf16[1,96,2048]{2,1,0:T(8,128)(2,1)S(1)} %get-tuple-element.28) | copy-start | bytes 1179652
  224.3 34.3 %copy-start.6 = (bf16[1,96,2048]{2,1,0:T(8,128)(2,1)S(1)}, bf16[1,96,2048]{2,1,0:T(8,128)(2,1)}, u32[]{:S(2)}) copy-start(bf16[1,96,2048]{2,1,0:T(8,128)(2,1)} %copy-done.5) | copy-start | bytes 1179652
  226.3 163.6 %all-reduce.5.cloned.1.call-start = ((), (), s32[]{:S(2)}) async-start(), calls=%async_computation.4 | async-start | bytes 1572864 | tf_op jit(solution)/shard_map/psum | solution.py:172
  228.6 84.0 %copy-start.27 = (f32[96,96]{1,0:T(8,128)}, f32[96,96]{1,0:T(8,128)S(1)}, u32[]{:S(2)}) copy-start(f32[96,96]{1,0:T(8,128)S(1)} %fusion.53) | copy-start | bytes 110596
  258.6 40.8 %copy-start.16 = (bf16[2,96,2048]{2,1,0:T(8,128)(2,1)S(1)}, bf16[2,96,2048]{2,1,0:T(8,128)(2,1)}, u32[]{:S(2)}) copy-start(bf16[2,96,2048]{2,1,0:T(8,128)(2,1)} %param.11) | copy-start | bytes 2359300
  259.8 12.8 %copy-start.13 = (bf16[96,2048]{1,0:T(8,128)(2,1)}, bf16[96,2048]{1,0:T(8,128)(2,1)S(1)}, u32[]{:S(2)}) copy-start(bf16[96,2048]{1,0:T(8,128)(2,1)S(1)} %fusion.80) | copy-start | bytes 1179652
  259.8 40.0 %copy-start.21 = (bf16[96,2048]{1,0:T(8,128)(2,1)S(1)}, bf16[96,2048]{1,0:T(8,128)(2,1)}, u32[]{:S(2)}) copy-start(bf16[96,2048]{1,0:T(8,128)(2,1)} %get-tuple-element.37) | copy-start | bytes 1179652
  259.8 39.6 %collective-permute-start = (bf16[96,2048]{1,0:T(8,128)(2,1)S(1)}, bf16[96,2048]{1,0:T(8,128)(2,1)S(1)}, u32[]{:S(2)}, u32[]{:S(2)}) collective-permute-start(bf16[96,2048]{1,0:T(8,128)(2,1)S(1)} %fusion.80), channel_id=1, source_target_pairs={{0,32},{32,64},{64,96},{96,128},{128,160},{160,192},{192,224},{224... | collective-permute-start | bytes 1179656 | tf_op jit(solution)/shard_map/ppermute | solution.py:15
  269.8 43.7 %collective-permute-start.1 = (bf16[96,2048]{1,0:T(8,128)(2,1)}, bf16[96,2048]{1,0:T(8,128)(2,1)}, u32[]{:S(2)}, u32[]{:S(2)}) collective-permute-start(bf16[96,2048]{1,0:T(8,128)(2,1)} %add_convert_fusion), channel_id=1, source_target_pairs={{32,0},{64,32},{96,64},{128,96},{160,128},{192,160},{224,192},{256... | collective-permute-start | bytes 1179656 | tf_op jit(solution)/shard_map/ppermute | solution.py:15
  310.0 3.5 copy-start.18
  317.8 4.4 copy-start.12
  317.8 6.1 %copy-start.26 = (f32[4,96,96]{2,1,0:T(8,128)S(1)}, f32[4,96,96]{2,1,0:T(8,128)}, u32[]{:S(2)}) copy-start(f32[4,96,96]{2,1,0:T(8,128)} %copy-done.25) | copy-start | bytes 442372
  317.8 6.1 %copy-start.28 = (f32[96,96]{1,0:T(8,128)S(1)}, f32[96,96]{1,0:T(8,128)}, u32[]{:S(2)}) copy-start(f32[96,96]{1,0:T(8,128)} %copy-done.27) | copy-start | bytes 110596
  327.4 6.3 %copy-start.15 = (f32[1,96,4,1,128]{4,1,2,3,0:T(8,128)S(1)}, f32[1,96,4,1,128]{4,1,2,3,0:T(8,128)}, u32[]{:S(2)}) copy-start(f32[1,96,4,1,128]{4,1,2,3,0:T(8,128)} %get-tuple-element.39) | copy-start | bytes 589828
  338.7 6.8 %copy-start.2 = (bf16[1,2,96,2048]{3,2,1,0:T(8,128)(2,1)S(1)}, bf16[1,2,96,2048]{3,2,1,0:T(8,128)(2,1)}, u32[]{:S(2)}) copy-start(bf16[1,2,96,2048]{3,2,1,0:T(8,128)(2,1)} %param.15) | copy-start | bytes 2359300
  338.7 7.8 %copy-start.20 = (bf16[1,96,4,128]{3,2,1,0:T(4,128)(2,1)S(1)}, bf16[1,96,4,128]{3,2,1,0:T(4,128)(2,1)}, u32[]{:S(2)}) copy-start(bf16[1,96,4,128]{3,2,1,0:T(4,128)(2,1)} %copy.53) | copy-start | bytes 294916
  347.7 137.4 %reduce-scatter.4.cloned.1.call-start = ((), (), s32[]{:S(2)}) async-start(), calls=%async_computation.3 | async-start | bytes 2228224
  352.2 38.6 %copy-start.4 = (bf16[96,2048]{1,0:T(8,128)(2,1)S(1)}, bf16[96,2048]{1,0:T(8,128)(2,1)}, u32[]{:S(2)}) copy-start(bf16[96,2048]{1,0:T(8,128)(2,1)} %copy-done.3) | copy-start | bytes 1179652
  (14 other events, 20.4 us)
Sparse Core Ops, SparseCore 0:
  10.0 81.4 all-gather.6
  93.7 105.7 all-gather.4
  226.4 32.1 all-reduce.6
  347.8 42.0 all-reduce.4
  392.6 92.4 reduce-scatter.3
where the time goes:
time: 494 us; the launch traced here: 493 us
  waiting for transfers between devices  364 us (74%)
  matrix products  45.3 us (9%)
  other arithmetic  30.4 us (6%)
  local copies, waits for them, and re-layouts  25.8 us (5%)
  between operations  17.2 us (3%)
  starting transfers between devices  11.1 us (2%)
    all_gather x1, waiting for transfers between devices, per_device(): in_full = lax.all_gather(in_weight[0], 'dp', axis=0, tiled=True)  105 us
    unnamed x6, waiting for transfers between devices  93.1 us
    all_gather x1, waiting for transfers between devices, per_device(): out_full = lax.all_gather(out_weight[0], 'dp', axis=1, tiled=True)  73.2 us
    psum x2, waiting for transfers between devices, per_device(): lax.psum(partial_sum.astype(jnp.bfloat16), 'cores').astype(jnp.float32)  65.7 us
    ppermute x2, waiting for transfers between devices, from_behind(): return lax.ppermute(x, axis, pairs)  26.8 us
    dot_general x2, matrix products, per_device(): jnp.einsum('sf,df->sd', grad_pre, in_full, preferred_element_type=jnp.flo...  13.3 us
    ppermute x2, starting transfers between devices, from_behind(): return lax.ppermute(x, axis, pairs)  10.9 us
    dot_general x2, matrix products, per_device(): pre_both = jnp.dot(both_normed, in_full, preferred_element_type=jnp.float32)  10.4 us
  transfers between devices with their start and end apart: 7, of which 6 were waited for; matrix products, arithmetic and copies ran while one was open for 7% of the time, Pallas kernels for 0%

commit v1 on v0

--- a/solution.py
+++ b/solution.py
@@ -2,6 +2,7 @@
 import jax.numpy as jnp
 from jax import lax
 from jax.sharding import PartitionSpec as P
+from jax.lax import all_gather
 
 HEAD_DIM = 128
 BLOCK = 24
@@ -169,7 +170,9 @@
         partial_sum = jnp.dot(
             gated_ahead.reshape(length, slab_rows), out_full, preferred_element_type=jnp.float32
         )
-        summed = lax.psum(partial_sum.astype(jnp.bfloat16), "cores").astype(jnp.float32)
+        summed = jnp.sum(
+            all_gather(partial_sum.astype(jnp.bfloat16), axis_name="cores"), axis=0
+        ).astype(jnp.float32)
         outgoing = (floats + summed).astype(jnp.bfloat16)
         ahead_out.append(lax.dynamic_slice_in_dim(outgoing, row_start, share, 0))
         if tick_no + 1 < ticks:

time: 494 us -> 466 us (0.943)
  the two profiles are of different devices: /device:TPU:8 before, /device:TPU:24 now
where the time goes in v1:
time: 466 us; the launch traced here: 465 us
  waiting for transfers between devices  320 us (69%)
  matrix products  46 us (10%)
  other arithmetic  35.1 us (8%)
  local copies, waits for them, and re-layouts  27.7 us (6%)
  between operations  17.2 us (4%)
  starting transfers between devices  13.7 us (3%)
  blocking collectives  5 us (1%)
    all_gather x1, waiting for transfers between devices, per_device(): in_full = lax.all_gather(in_weight[0], 'dp', axis=0, tiled=True)  105 us
    unnamed x6, waiting for transfers between devices  95.1 us
    all_gather x1, waiting for transfers between devices, per_device(): out_full = lax.all_gather(out_weight[0], 'dp', axis=1, tiled=True)  71.2 us
    psum x2, waiting for transfers between devices, per_device(): lax.psum(back_part.astype(jnp.bfloat16), 'cores').astype(jnp.float32)  27.2 us
    ppermute x2, waiting for transfers between devices, from_behind(): return lax.ppermute(x, axis, pairs)  21 us
    dot_general x2, matrix products, per_device(): jnp.einsum('sf,df->sd', grad_pre, in_full, preferred_element_type=jnp.flo...  13.5 us
    ppermute x2, starting transfers between devices, from_behind(): return lax.ppermute(x, axis, pairs)  13.3 us
    dot_general x2, matrix products, per_device(): pre_both = jnp.dot(both_normed, in_full, preferred_element_type=jnp.float32)  10.5 us
  transfers between devices with their start and end apart: 7, of which 7 were waited for; matrix products, arithmetic and copies ran while one was open for 13% of the time, Pallas kernels for 0%

profile of v1, /device:TPU:24, one launch (start us, length us, event | category | flops | bytes accessed | tf_op | source)
XLA Modules:
  0.0 464.5 jit_solution(10608705359505877777)
XLA Ops:
  20.2 71.2 %all-gather.9.cloned.1.call-done = bf16[1,512,2048]{2,1,0:T(8,128)(2,1)} async-done(((bf16[1,512,128]{2,1,0:T(8,128)(2,1)}), bf16[1,512,2048]{2,1,0:T(8,128)(2,1)}) %all-gather.9.cloned.1.call-update) | async-done | bytes 2097168 | tf_op jit(solution)/shard_map/all_gather | solution.py:131
  91.4 2.4 fusion.31
  93.8 105.4 %all-gather.7.cloned.1.call-done = bf16[1,2048,2048]{2,1,0:T(8,128)(2,1)} async-done(((bf16[1,128,2048]{2,1,0:T(8,128)(2,1)}), bf16[1,2048,2048]{2,1,0:T(8,128)(2,1)}) %all-gather.7.cloned.1.call-update) | async-done | bytes 8388624 | tf_op jit(solution)/shard_map/all_gather | solution.py:136
  199.2 5.2 %fusion.6 = f32[192,2048]{1,0:T(8,128)S(1)} fusion(bf16[1,2048,2048]{2,1,0:T(8,128)(2,1)} %all-gather.7.cloned.1.call-done, bf16[96,2048]{1,0:T(8,128)(2,1)S(1)} %get-tuple-element.48, bf16[96,2048]{1,0:T(8,128)(2,1)S(1)} %get-tuple-element.49), kind=kOutput, calls=%fused_computation.6 | convolution fusion | flops 1612185600 | bytes 10747904 | tf_op jit(solution)/shard_map/dot_general | solution.py:166
  214.4 2.6 fusion.156
  220.7 2.5 all-gather.2
  227.3 5.3 %collective-permute-start = (bf16[96,2048]{1,0:T(8,128)(2,1)}, bf16[96,2048]{1,0:T(8,128)(2,1)}, u32[]{:S(2)}, u32[]{:S(2)}) collective-permute-start(bf16[96,2048]{1,0:T(8,128)(2,1)} %fusion.80), channel_id=1, source_target_pairs={{0,32},{32,64},{64,96},{96,128},{128,160},{160,192},{192,224},{224... | collective-permute-start | bytes 1179656 | tf_op jit(solution)/shard_map/ppermute | solution.py:16
  235.2 2.4 stack.60
  237.6 6.8 %fusion.68 = (f32[96]{0:T(128)S(1)}, f32[96]{0:T(128)S(1)}, f32[96,2048]{1,0:T(8,128)S(1)}) fusion(f32[96]{0:T(128)S(1)} %add_rsqrt_fusion.6, bf16[1,2,96,2048]{3,2,1,0:T(8,128)(2,1)S(1)} %copy-done.1, bf16[1,2048,2048]{2,1,0:T(8,128)(2,1)} %all-gather.7.cloned.1.call-done, f32[96,2048]{1,0:T(8,128)} %stack.60, f32[192,2048]{1,0:T(8,128)} %copy-done.6), kind=kOutput, calls=%fused_computation.86 | convolution fusion | flops 808451840 | bytes 11535488 | tf_op jit(solution)/shard_map/sf,df->sd/dot_general | solution.py:187
  245.9 8.0 %collective-permute-done = bf16[96,2048]{1,0:T(8,128)(2,1)} collective-permute-done((bf16[96,2048]{1,0:T(8,128)(2,1)}, bf16[96,2048]{1,0:T(8,128)(2,1)}, u32[]{:S(2)}, u32[]{:S(2)}) %collective-permute-start) | collective-permute-done | bytes 393248 | tf_op jit(solution)/shard_map/ppermute | solution.py:16
  255.3 5.3 %fusion.4 = f32[192,2048]{1,0:T(8,128)S(1)} fusion(bf16[1,2048,2048]{2,1,0:T(8,128)(2,1)} %all-gather.7.cloned.1.call-done, bf16[96,2048]{1,0:T(8,128)(2,1)S(1)} %copy-done.13, bf16[96,2048]{1,0:T(8,128)(2,1)S(1)} %multiply_convert_fusion.2), kind=kOutput, calls=%fused_computation.4 | convolution fusion | flops 1612185600 | bytes 10747904 | tf_op jit(solution)/shard_map/dot_general | solution.py:166
  263.1 2.5 reshape.826
  265.7 2.5 fusion.152
  268.2 8.4 %all-reduce.3.cloned.1.call-done = bf16[96,2048]{1,0:T(8,128)(2,1)} async-done(((bf16[96,2048]{1,0:T(8,128)(2,1)}), bf16[96,2048]{1,0:T(8,128)(2,1)}) %all-reduce.3.cloned.1.call-update) | async-done | bytes 393232 | tf_op jit(solution)/shard_map/psum | solution.py:192
  277.8 8.0 %collective-permute-start.1 = (bf16[96,2048]{1,0:T(8,128)(2,1)S(1)}, bf16[96,2048]{1,0:T(8,128)(2,1)S(1)}, u32[]{:S(2)}, u32[]{:S(2)}) collective-permute-start(bf16[96,2048]{1,0:T(8,128)(2,1)S(1)} %add_convert_fusion), channel_id=1, source_target_pairs={{32,0},{64,32},{96,64},{128,96},{160,128},{192,160},{224,192},{256... | collective-permute-start | bytes 1179656 | tf_op jit(solution)/shard_map/ppermute | solution.py:16
  288.7 13.0 %collective-permute-done.1 = bf16[96,2048]{1,0:T(8,128)(2,1)S(1)} collective-permute-done((bf16[96,2048]{1,0:T(8,128)(2,1)S(1)}, bf16[96,2048]{1,0:T(8,128)(2,1)S(1)}, u32[]{:S(2)}, u32[]{:S(2)}) %collective-permute-start.1) | collective-permute-done | bytes 393248 | tf_op jit(solution)/shard_map/ppermute | solution.py:16
  311.4 2.3 stack.67
  313.7 6.8 %fusion.73 = (f32[96]{0:T(128)S(1)}, f32[96,2048]{1,0:T(8,128)S(1)}) fusion(f32[96]{0:T(128)S(1)} %add_rsqrt_fusion.4, bf16[1,2,96,2048]{3,2,1,0:T(8,128)(2,1)} %param.15, bf16[1,2048,2048]{2,1,0:T(8,128)(2,1)} %all-gather.7.cloned.1.call-done, f32[96,2048]{1,0:T(8,128)} %stack.67, f32[192,2048]{1,0:T(8,128)} %copy-done.7), kind=kOutput, calls=%fused_computation.91 | convolution fusion | flops 807862144 | bytes 11141888 | tf_op jit(solution)/shard_map/sf,df->sd/dot_general | solution.py:187
  321.8 3.0 convolution_convert_fusion
  324.8 3.9 copy.74
  330.8 2.6 reshape.822
  338.5 2.5 all-gather.3
  342.0 18.8 %all-reduce.5.cloned.1.call-done = bf16[96,2048]{1,0:T(8,128)(2,1)} async-done(((bf16[96,2048]{1,0:T(8,128)(2,1)}), bf16[96,2048]{1,0:T(8,128)(2,1)}) %all-reduce.5.cloned.1.call-update) | async-done | bytes 393232 | tf_op jit(solution)/shard_map/psum | solution.py:192
  362.6 93.6 %reduce-scatter.4.cloned.1.call-done = bf16[128,512]{1,0:T(8,128)(2,1)} async-done(((bf16[2048,512]{1,0:T(8,128)(2,1)}), bf16[128,512]{1,0:T(8,128)(2,1)}) %reduce-scatter.4.cloned.1.call-update) | async-done | bytes 131088
  (141 shorter events, 62.3 us)
Async XLA Ops:
  7.2 12.8 %copy-start.1 = (bf16[1,2,96,2048]{3,2,1,0:T(8,128)(2,1)S(1)}, bf16[1,2,96,2048]{3,2,1,0:T(8,128)(2,1)}, u32[]{:S(2)}) copy-start(bf16[1,2,96,2048]{3,2,1,0:T(8,128)(2,1)} %param.15) | copy-start | bytes 2359300
  7.2 12.7 %copy-start.16 = (bf16[1,96,2048]{2,1,0:T(8,128)(2,1)S(1)}, bf16[1,96,2048]{2,1,0:T(8,128)(2,1)}, u32[]{:S(2)}) copy-start(bf16[1,96,2048]{2,1,0:T(8,128)(2,1)} %param.14) | copy-start | bytes 1179652
  7.2 12.7 %copy-start.11 = (bf16[2,96,2048]{2,1,0:T(8,128)(2,1)S(1)}, bf16[2,96,2048]{2,1,0:T(8,128)(2,1)}, u32[]{:S(2)}) copy-start(bf16[2,96,2048]{2,1,0:T(8,128)(2,1)} %param.13) | copy-start | bytes 2359300
  7.2 84.2 %all-gather.9.cloned.1.call-start = ((), (), s32[]{:S(2)}) async-start(), calls=%async_computation.4 | async-start | bytes 2228224 | tf_op jit(solution)/shard_map/all_gather | solution.py:131
  7.9 191.3 %all-gather.7.cloned.1.call-start = ((), (), s32[]{:S(2)}) async-start(), calls=%async_computation.3 | async-start | bytes 8912896 | tf_op jit(solution)/shard_map/all_gather | solution.py:136
  8.7 267.9 %all-reduce.3.cloned.1.call-start = ((), (), s32[]{:S(2)}) async-start(), calls=%async_computation.1 | async-start | bytes 786432 | tf_op jit(solution)/shard_map/psum | solution.py:192
  17.9 75.8 %copy-start.5 = (bf16[1,96,2048]{2,1,0:T(8,128)(2,1)}, bf16[1,96,2048]{2,1,0:T(8,128)(2,1)S(1)}, u32[]{:S(2)}) copy-start(bf16[1,96,2048]{2,1,0:T(8,128)(2,1)S(1)} %get-tuple-element.24) | copy-start | bytes 1179652
  19.4 188.6 %copy-start.19 = (f32[96,96]{1,0:T(8,128)}, f32[96,96]{1,0:T(8,128)S(1)}, u32[]{:S(2)}) copy-start(f32[96,96]{1,0:T(8,128)S(1)} %fusion.48) | copy-start | bytes 110596
  208.3 3.7 copy-start.20
  214.4 5.8 %copy-start = (bf16[1,512,2048]{2,1,0:T(8,128)(2,1)S(1)}, bf16[1,512,2048]{2,1,0:T(8,128)(2,1)}, u32[]{:S(2)}) copy-start(bf16[1,512,2048]{2,1,0:T(8,128)(2,1)} %all-gather.9.cloned.1.call-done) | copy-start | bytes 6291460
  227.3 26.5 %collective-permute-start = (bf16[96,2048]{1,0:T(8,128)(2,1)}, bf16[96,2048]{1,0:T(8,128)(2,1)}, u32[]{:S(2)}, u32[]{:S(2)}) collective-permute-start(bf16[96,2048]{1,0:T(8,128)(2,1)} %fusion.80), channel_id=1, source_target_pairs={{0,32},{32,64},{64,96},{96,128},{128,160},{160,192},{192,224},{224... | collective-permute-start | bytes 1179656 | tf_op jit(solution)/shard_map/ppermute | solution.py:16
  245.6 115.2 %all-reduce.5.cloned.1.call-start = ((), (), s32[]{:S(2)}) async-start(), calls=%async_computation.2 | async-start | bytes 786432 | tf_op jit(solution)/shard_map/psum | solution.py:192
  245.8 9.5 %copy-start.13 = (bf16[96,2048]{1,0:T(8,128)(2,1)S(1)}, bf16[96,2048]{1,0:T(8,128)(2,1)}, u32[]{:S(2)}) copy-start(bf16[96,2048]{1,0:T(8,128)(2,1)} %get-tuple-element.34) | copy-start | bytes 1179652
  276.6 25.2 %copy-start.12 = (bf16[2,96,2048]{2,1,0:T(8,128)(2,1)S(1)}, bf16[2,96,2048]{2,1,0:T(8,128)(2,1)}, u32[]{:S(2)}) copy-start(bf16[2,96,2048]{2,1,0:T(8,128)(2,1)} %param.13) | copy-start | bytes 2359300
  277.8 11.0 %copy-start.9 = (bf16[96,2048]{1,0:T(8,128)(2,1)}, bf16[96,2048]{1,0:T(8,128)(2,1)S(1)}, u32[]{:S(2)}) copy-start(bf16[96,2048]{1,0:T(8,128)(2,1)S(1)} %add_convert_fusion) | copy-start | bytes 1179652
  277.8 24.0 %collective-permute-start.1 = (bf16[96,2048]{1,0:T(8,128)(2,1)S(1)}, bf16[96,2048]{1,0:T(8,128)(2,1)S(1)}, u32[]{:S(2)}, u32[]{:S(2)}) collective-permute-start(bf16[96,2048]{1,0:T(8,128)(2,1)S(1)} %add_convert_fusion), channel_id=1, source_target_pairs={{32,0},{64,32},{96,64},{128,96},{160,128},{192,160},{224,192},{256... | collective-permute-start | bytes 1179656 | tf_op jit(solution)/shard_map/ppermute | solution.py:16
  286.9 1.9 copy-start.17
  305.0 4.2 copy-start.8
  305.0 4.6 copy-start.18
  313.7 6.8 %copy-start.2 = (bf16[1,2,96,2048]{3,2,1,0:T(8,128)(2,1)S(1)}, bf16[1,2,96,2048]{3,2,1,0:T(8,128)(2,1)}, u32[]{:S(2)}) copy-start(bf16[1,2,96,2048]{3,2,1,0:T(8,128)(2,1)} %param.15) | copy-start | bytes 2359300
  313.7 7.9 %copy-start.14 = (bf16[1,96,4,128]{3,1,2,0:T(8,128)(2,1)S(1)}, bf16[1,96,4,128]{3,1,2,0:T(8,128)(2,1)}, u32[]{:S(2)}) copy-start(bf16[1,96,4,128]{3,1,2,0:T(8,128)(2,1)} %get-tuple-element.29) | copy-start | bytes 294916
  321.5 134.7 %reduce-scatter.4.cloned.1.call-start = ((), (), s32[]{:S(2)}) async-start(), calls=%async_computation.5 | async-start | bytes 2228224
  338.4 2.7 copy-start.10
  338.5 22.4 %copy-start.4 = (bf16[96,2048]{1,0:T(8,128)(2,1)S(1)}, bf16[96,2048]{1,0:T(8,128)(2,1)}, u32[]{:S(2)}) copy-start(bf16[96,2048]{1,0:T(8,128)(2,1)} %copy-done.3) | copy-start | bytes 1179652
  (4 other events, 4.6 us)
Sparse Core Ops, SparseCore 0:
  10.0 81.2 all-gather.8
  93.5 105.7 all-gather.6
  245.7 30.7 all-reduce.2
  321.6 39.1 all-reduce.4
  363.5 92.6 reduce-scatter.3
